TPU v7x, 128 devices: a whole 4x4x4 slice. The times are simulated.
128 devices in a mesh: segment: 2 (over core), fsdp: 32 (over x, y_lo, z), dp: 2 (over y_hi).
Axes of the slice: x: 4, y: 4 (y_hi: 2, y_lo: 2; y = y_hi * 2 + y_lo), z: 4, core: 2. Of those that a mesh axis runs over, the one named last changes fastest.
Arguments:
- hooks: bfloat16 [2, 4, 256, 64, 6144], P('segment', 'dp', 'fsdp'), may hold values from -6 to 6
- proj_weight: bfloat16 [2, 6144, 256], P('segment', 'fsdp'), may hold values from -0.078125 to 0.078125
- conv_weight: bfloat16 [2, 2, 2304, 256], P('segment', None, 'fsdp'), may hold values from -0.125 to 0.125
- head_weight: bfloat16 [3, 256], replicated, may hold values from -0.375 to 0.375
- light_color: float32 [25, 3], replicated, may hold values from 0.3 to 1.5
- illum: int32 [4, 4], P('dp'), may hold values from 0 to 24
- offsets: int32 [4, 4, 2], P('dp'), may hold values from 0 to 32
- photos: bfloat16 [4, 4, 3, 96, 96], P('dp'), may hold values from 0 to 10
Outputs:
- grad_proj: float32 [2, 6144, 256], P('segment', 'fsdp')
- grad_conv: float32 [2, 2, 2304, 256], P('segment', None, 'fsdp')
- grad_head: float32 [3, 256], replicated
- loss: float32 [], replicated
All inputs are finite; a program needn't handle non-finite values.
Results may differ from a plain program's by a relative error of at most 0.018.
Values may be sent and summed in bfloat16 or wider, within the bound.
A program may use at most 128 MiB of HBM per device.

v0:
```python
import jax
import jax.numpy as jnp
from jax import lax
from jax.sharding import PartitionSpec as P

LOSS_SCALE = 8192.0


def extended(shard, sides, width):
    for axis, dim in sides:
        size, length = (lax.axis_size(axis), shard.shape[dim])
        up = [(i, (i + 1) % size) for i in range(size - 1)]
        down = [(j, i) for i, j in up]
        last = lax.slice_in_dim(shard, length - width, length, axis=dim)
        initial = lax.slice_in_dim(shard, 0, width, axis=dim)
        before = lax.ppermute(last, axis, up)
        after = lax.ppermute(initial, axis, down)
        shard = jnp.concatenate([before, shard, after], axis=dim)
    return shard


def shifted(shard, axis, by):
    size = lax.axis_size(axis)
    pairs = [(i, i + by) for i in range(size) if 0 <= i + by < size]
    return lax.ppermute(shard, axis, pairs)


def activate(values):
    return jax.nn.gelu(values, approximate=True)


def activate_slope(values):
    return jax.vjp(activate, values)[1](jnp.ones_like(values))[0]


def patches(field):
    rows_here, cols_here, channels = (field.shape[1], field.shape[2], field.shape[3])
    padded = extended(field, (("fsdp", 1),), 1)
    row_base = lax.axis_index("fsdp") * rows_here % cols_here
    upper = jnp.where(row_base == 0, jnp.zeros_like(padded[:, :1]), padded[:, :1])
    lower = jnp.where(
        row_base + rows_here == cols_here, jnp.zeros_like(padded[:, -1:]), padded[:, -1:]
    )
    padded = jnp.concatenate([upper, padded[:, 1:-1], lower], axis=1)
    padded = jnp.pad(padded, ((0, 0), (0, 0), (1, 1), (0, 0)))
    pieces = [
        padded[:, i : i + rows_here, j : j + cols_here, :] for i in range(3) for j in range(3)
    ]
    return jnp.concatenate(pieces, axis=-1).reshape(-1, 9 * channels)


def contract_rows(left, right):
    return lax.dot_general(
        left, right, (((0,), (0,)), ((), ())), preferred_element_type=jnp.float32
    )


def flipped(kernel):
    channels = kernel.shape[1]
    grid_form = kernel.reshape(3, 3, channels, channels)[::-1, ::-1]
    return jnp.swapaxes(grid_form, 2, 3).reshape(9 * channels, channels)


def section_parts(segment_in, first_conv, second_conv):
    channels = segment_in.shape[-1]
    first_in = activate(segment_in.astype(jnp.float32)).astype(jnp.bfloat16)
    first_patches = patches(first_in)
    hidden = jnp.dot(first_patches, first_conv, preferred_element_type=jnp.float32)
    second_in = activate(hidden).astype(jnp.bfloat16).reshape(segment_in.shape)
    second_patches = patches(second_in)
    update = jnp.dot(second_patches, second_conv, preferred_element_type=jnp.float32)
    output = (segment_in.reshape(-1, channels).astype(jnp.float32) + update).astype(jnp.bfloat16)
    return (output.reshape(segment_in.shape), first_patches, hidden, second_patches)


def section_back(segment_in, out_grad, first_conv, second_conv, first_flip, second_flip):
    channels = segment_in.shape[-1]
    output, first_patches, hidden, second_patches = section_parts(
        segment_in, first_conv, second_conv
    )
    out_rows = out_grad.reshape(-1, channels)
    second_grad = jnp.dot(patches(out_grad), second_flip, preferred_element_type=jnp.float32)
    hidden_grad = (second_grad * activate_slope(hidden)).astype(jnp.bfloat16)
    first_grad = jnp.dot(
        patches(hidden_grad.reshape(segment_in.shape)),
        first_flip,
        preferred_element_type=jnp.float32,
    )
    slope = activate_slope(segment_in.reshape(-1, channels).astype(jnp.float32))
    in_grad = (
        (out_rows.astype(jnp.float32) + first_grad * slope)
        .astype(jnp.bfloat16)
        .reshape(segment_in.shape)
    )
    return (
        in_grad,
        contract_rows(first_patches, hidden_grad),
        contract_rows(second_patches, out_rows),
    )


def head_loss(output, head_weight, tints, targets, factor):
    channels = output.shape[-1]
    out_rows = output.reshape(-1, channels)
    logits = lax.dot_general(
        head_weight, out_rows, (((1,), (1,)), ((), ())), preferred_element_type=jnp.float32
    )
    albedo = jax.nn.sigmoid(logits.reshape(targets.shape))
    tint = jnp.transpose(tints)[:, :, None, None]
    mismatch = albedo * tint - targets
    squares = jnp.sum(mismatch * mismatch)
    logit_grad = (
        (factor * mismatch * tint * albedo * (1.0 - albedo)).astype(jnp.bfloat16).reshape(3, -1)
    )
    head_grad = lax.dot_general(
        logit_grad, out_rows, (((1,), (0,)), ((), ())), preferred_element_type=jnp.float32
    )
    out_grad = lax.dot_general(
        logit_grad, head_weight, (((0,), (0,)), ((), ())), preferred_element_type=jnp.float32
    )
    return (squares, head_grad, out_grad.astype(jnp.bfloat16).reshape(output.shape))


def crop_tints(illum, light_color):
    lights = light_color.shape[0]
    onehot = (illum[..., None] == jnp.arange(lights, dtype=jnp.int32)).astype(jnp.float32)
    return jnp.dot(onehot.reshape(-1, lights), light_color, precision=lax.Precision.HIGHEST)


def crop_targets(photos, offsets, row_base, rows_here, cols_here):

    def one_crop(picture, offset):
        start = (jnp.zeros((), jnp.int32), offset[0] + row_base, offset[1])
        return lax.dynamic_slice(picture, start, (3, rows_here, cols_here))

    cut = jax.vmap(jax.vmap(one_crop))(photos, offsets).astype(jnp.float32)
    return jnp.moveaxis(cut, 2, 0)


def fetch_convs(conv_weight):
    gathered = lax.all_gather(conv_weight[0], "fsdp", axis=1, tiled=True)
    return (gathered[0], gathered[1])


def pass_on(field):
    return shifted(field, "segment", 1)


def pass_back(field):
    return shifted(field, "segment", -1)


def body(hooks, proj_weight, conv_weight, head_weight, light_color, illum, offsets, photos):
    segments = lax.axis_size("segment")
    segment_index = lax.axis_index("segment")
    is_last = segment_index == segments - 1
    micro_count, band_rows, grid_cols, model_width = (
        hooks.shape[1],
        hooks.shape[2],
        hooks.shape[3],
        hooks.shape[4],
    )
    crop_count = 1
    channels = proj_weight.shape[2]
    tokens = hooks[0].reshape(-1, model_width)
    first_global = lax.axis_index("fsdp") * band_rows
    crop_here = first_global // grid_cols
    row_base = first_global % grid_cols
    columns = tokens
    projected = jnp.dot(
        columns,
        lax.all_gather(proj_weight[0], "fsdp", axis=0, tiled=True),
        preferred_element_type=jnp.float32,
    )
    projected = projected.astype(jnp.bfloat16).reshape(
        micro_count, crop_count, band_rows, grid_cols, channels
    )
    first_conv, second_conv = fetch_convs(conv_weight)
    micro_shape = (crop_count, band_rows, grid_cols, channels)
    flat_shape = (micro_count * crop_count, band_rows, grid_cols, channels)
    flat_proj = projected.reshape(flat_shape)
    incoming = jnp.zeros_like(flat_proj)
    for p in range(segments):
        segment_in = (flat_proj.astype(jnp.float32) + incoming.astype(jnp.float32)).astype(
            jnp.bfloat16
        )
        output = section_parts(segment_in, first_conv, second_conv)[0]
        if p + 1 < segments:
            incoming = pass_on(output)
    inputs_all = segment_in.reshape((micro_count,) + micro_shape)
    outputs_all = output.reshape((micro_count,) + micro_shape)
    illum_here = lax.dynamic_slice_in_dim(illum, crop_here, 1, 1)
    offsets_here = lax.dynamic_slice_in_dim(offsets, crop_here, 1, 1)
    photos_here = lax.dynamic_slice_in_dim(photos, crop_here, 1, 1)
    tints = crop_tints(illum_here, light_color)
    targets = crop_targets(photos_here, offsets_here, row_base, band_rows, grid_cols)
    targets = targets.reshape(3, micro_count * crop_count, band_rows, grid_cols)
    npix = 3 * micro_count * lax.axis_size("dp") * band_rows * lax.axis_size("fsdp") * grid_cols
    factor = 2.0 * LOSS_SCALE / npix
    squares, head_grad, out_grads = head_loss(
        outputs_all.reshape(flat_shape), head_weight, tints, targets, factor
    )
    out_grads = out_grads.reshape((micro_count,) + micro_shape)
    back_first, back_second = fetch_convs(conv_weight)
    first_flip = flipped(back_first)
    second_flip = flipped(back_second)
    flat_in = inputs_all.reshape(flat_shape)
    flat_grads = out_grads.reshape(flat_shape)
    received = jnp.zeros_like(flat_grads)
    for p in range(segments):
        out_grad = jnp.where(is_last, flat_grads, received)
        in_grad, first_sum, second_sum = section_back(
            flat_in, out_grad, back_first, back_second, first_flip, second_flip
        )
        if p + 1 < segments:
            received = pass_back(in_grad)
    grad_rows = in_grad.reshape(-1, channels)
    conv_sums = jnp.concatenate([first_sum, second_sum], axis=1)
    columns = tokens
    proj_part = lax.psum_scatter(
        contract_rows(columns, grad_rows), "fsdp", scatter_dimension=0, tiled=True
    )
    conv_part = lax.psum_scatter(conv_sums, "fsdp", scatter_dimension=0, tiled=True)
    proj_part, conv_part = lax.psum((proj_part, conv_part), "dp")
    loss_term = jnp.where(is_last, squares, 0.0)
    head_term = jnp.where(is_last, head_grad, 0.0)
    head_total, square_total = lax.psum((head_term, loss_term), ("segment", "fsdp", "dp"))
    grad_conv = jnp.stack([conv_part[:, :channels], conv_part[:, channels:]])[None]
    return (proj_part[None], grad_conv, head_total, square_total / npix)


def solution(mesh):
    placed = (
        P("segment", "dp", "fsdp", None, None),
        P("segment", "fsdp", None),
        P("segment", None, "fsdp", None),
        P(),
        P(),
        P("dp", None),
        P("dp", None, None),
        P("dp", None, None, None, None),
    )
    return jax.shard_map(
        body,
        mesh=mesh,
        in_specs=placed,
        out_specs=(P("segment", "fsdp", None), P("segment", None, "fsdp", None), P(), P()),
        check_vma=False,
    )
```

profile of v0, /device:TPU:1, one launch (start us, length us, event | category | flops | bytes accessed | tf_op | source)
XLA Modules:
  0.0 882.3 jit_solution(2431889212769604529)
XLA Ops:
  9.6 138.4 %all-gather.5.cloned.1.call-done = bf16[1,6144,256]{2,1,0:T(8,128)(2,1)} async-done(((bf16[1,192,256]{2,1,0:T(8,128)(2,1)}), bf16[1,6144,256]{2,1,0:T(8,128)(2,1)}) %all-gather.5.cloned.1.call-update) | async-done | bytes 3145744 | tf_op jit(solution)/shard_map/all_gather | solution.py:172
  147.9 7.3 fusion.8
  157.1 4.0 collective-permute-start
  171.4 132.0 %all-gather.7.cloned.1.call-done = bf16[1,2,2304,256]{3,2,1,0:T(8,128)(2,1)} async-done(((bf16[1,2,72,256]{3,2,1,0:T(8,128)(2,1)}), bf16[1,2,2304,256]{3,2,1,0:T(8,128)(2,1)}) %all-gather.7.cloned.1.call-update) | async-done | bytes 2359312 | tf_op jit(solution)/shard_map/all_gather | solution.py:141
  303.4 4.2 fusion.54
  307.6 3.0 collective-permute-start.2
  312.0 4.4 collective-permute-done.3
  321.9 12.9 %copy.50 = bf16[2,1,3,96,96]{2,1,0,4,3:T(2,128)(2,1)} copy(bf16[2,1,3,96,96]{4,3,2,1,0:T(8,128)(2,1)S(1)} %constant_dynamic-slice_fusion.2) | data formatting | bytes 221184
  334.8 3.3 gather_fusion
  339.5 5.5 collective-permute-done.4
  347.1 1.8 fusion.92
  350.7 3.2 collective-permute-done.6
  355.9 2.5 multiply_convert_fusion
  358.4 1.9 collective-permute-start.7
  361.7 3.6 collective-permute-done.8
  375.8 4.1 collective-permute-start.9
  385.2 3.6 collective-permute-start.11
  391.0 3.7 collective-permute-done.12
  397.4 23.5 %collective-permute-start.13 = (bf16[2,8,64,256]{3,2,1,0:T(8,128)(2,1)S(1)}, bf16[2,8,64,256]{3,2,1,0:T(8,128)(2,1)S(1)}, u32[]{:S(2)}, u32[]{:S(2)}) collective-permute-start(bf16[2,8,64,256]{3,2,1,0:T(8,128)(2,1)S(1)} %bitcast.225), channel_id=1, source_target_pairs={{64,0},{65,1},{66,2},{67,3},{68,4},{69,5},{70,6},{71,7},{72,8},{73... | collective-permute-start | bytes 1572872 | tf_op jit(solution)/shard_map/ppermute | solution.py:25
  422.4 4.8 collective-permute-start.14
  430.1 4.8 collective-permute-done.15
  436.1 1.8 fusion.14
  439.7 2.5 pad_maximum_fusion
  442.2 6.1 copy.48
  448.4 5.8 collective-permute-start.16
  455.7 3.5 collective-permute-done.17
  460.5 2.2 copy-done.11
  462.7 16.0 %convolution_bitcast_fusion = f32[6144,256]{0,1:T(8,128)} fusion(bf16[1024,6144]{1,0:T(8,128)(2,1)} %bitcast.223, bf16[1024,256]{1,0:T(8,128)(2,1)S(1)} %bitcast.150, f32[1024,256]{1,0:T(8,128)S(1)} %fusion.36, bf16[1024,2304]{1,0:T(8,128)(2,1)} %copy-done.11, bf16[2304,256]{1,0:T(8,128)(2,1)S(1)} %bitcast.207), kind=kOutput, calls=%fused_computation.1 | convolution fusion | flops 4430233600 | bytes 26345472 | tf_op jit(solution)/shard_map/dot_general | solution.py:53
  478.7 6.6 copy.46
  485.7 119.6 %reduce-scatter.9.cloned.1.call-done = f32[72,512]{1,0:T(8,128)} async-done(((f32[2304,512]{1,0:T(8,128)}), f32[72,512]{1,0:T(8,128)}) %reduce-scatter.9.cloned.1.call-update) | async-done | bytes 147472
  607.1 171.1 %reduce-scatter.7.cloned.1.call-done = f32[192,256]{1,0:T(8,128)} async-done(((f32[6144,256]{1,0:T(8,128)}), f32[192,256]{1,0:T(8,128)}) %reduce-scatter.7.cloned.1.call-update) | async-done | bytes 196624
  782.0 88.2 %all-reduce.8 = (f32[3,256]{1,0:T(4,128)}, f32[]{:T(128)}) all-reduce(f32[3,256]{1,0:T(4,128)S(1)} %convolution_select_fusion, f32[]{:T(128)S(6)} %select_n.191), channel_id=1, replica_groups=mesh['segment'=2,'fsdp'=32,'dp'=2] {'segment','fsdp','dp'}, use_global_device_ids=true, to_apply=%region_4.5 | all-reduce | flops 769 | bytes 6152 | tf_op jit(solution)/shard_map/psum | solution.py:227
  (240 shorter events, 68.9 us)
Async XLA Ops:
  7.2 303.4 %copy-start = (bf16[2,4,3,96,96]{4,3,2,1,0:T(8,128)(2,1)S(1)}, bf16[2,4,3,96,96]{4,3,2,1,0:T(8,128)(2,1)}, u32[]{:S(2)}) copy-start(bf16[2,4,3,96,96]{4,3,2,1,0:T(8,128)(2,1)} %param.15) | copy-start | bytes 1327108
  7.2 140.8 %all-gather.5.cloned.1.call-start = ((), (), s32[]{:S(2)}) async-start(), calls=%async_computation.2 | async-start | bytes 3244032 | tf_op jit(solution)/shard_map/all_gather | solution.py:172
  7.9 295.4 %all-gather.7.cloned.1.call-start = ((), (), s32[]{:S(2)}) async-start(), calls=%async_computation.3 | async-start | bytes 2433024 | tf_op jit(solution)/shard_map/all_gather | solution.py:141
  8.7 596.7 %reduce-scatter.9.cloned.1.call-start = ((), (), s32[]{:S(2)}) async-start(), calls=%async_computation.5 | async-start | bytes 4866048
  155.6 5.4 collective-permute-start.1
  157.1 5.3 collective-permute-start
  307.6 4.4 collective-permute-start.2
  310.6 5.7 collective-permute-start.3
  320.4 24.6 %collective-permute-start.4 = (bf16[2,8,64,256]{3,2,1,0:T(8,128)(2,1)S(1)}, bf16[2,8,64,256]{3,2,1,0:T(8,128)(2,1)S(1)}, u32[]{:S(2)}, u32[]{:S(2)}) collective-permute-start(bf16[2,8,64,256]{3,2,1,0:T(8,128)(2,1)S(1)} %bitcast.224), channel_id=1, source_target_pairs={{0,64},{1,65},{2,66},{3,67},{4,68},{5,69},{6,70},{7,71},{8,72},{9,... | collective-permute-start | bytes 1572872 | tf_op jit(solution)/shard_map/ppermute | solution.py:25
  321.9 16.8 %copy-start.15 = (s32[2,4]{1,0:T(2,128)S(1)}, s32[2,4]{1,0:T(2,128)}, u32[]{:S(2)}) copy-start(s32[2,4]{1,0:T(2,128)} %param.13) | copy-start | bytes 100
  321.9 16.9 %copy-start.16 = (f32[25,3]{0,1:T(4,128)S(1)}, f32[25,3]{0,1:T(4,128)}, u32[]{:S(2)}) copy-start(f32[25,3]{0,1:T(4,128)} %param.12) | copy-start | bytes 904
  345.4 23.8 %copy-start.2 = (f32[2,8,64,256]{3,2,1,0:T(8,128)}, f32[2,8,64,256]{3,2,1,0:T(8,128)S(1)}, u32[]{:S(2)}) copy-start(f32[2,8,64,256]{3,2,1,0:T(8,128)S(1)} %get-tuple-element.29) | copy-start | bytes 3145732
  345.4 5.2 collective-permute-start.5
  348.9 5.0 collective-permute-start.6
  358.4 3.3 collective-permute-start.7
  360.3 5.0 collective-permute-start.8
  372.1 7.7 collective-permute-start.10
  375.8 5.7 collective-permute-start.9
  385.2 5.7 collective-permute-start.11
  389.5 5.2 collective-permute-start.12
  396.0 32.6 %slice-start = ((s8[4718592]{0:T(1024)(128)(4,1)}), s8[524288]{0:T(1024)(128)(4,1)S(1)}, s32[]{:S(2)}) async-start(s8[4718592]{0:T(1024)(128)(4,1)} %bitcast.211), calls=%async_computation.7 | async-start | bytes 1048576
  396.0 32.6 %slice-start.1 = ((s8[4718592]{0:T(1024)(128)(4,1)}), s8[4194304]{0:T(1024)(128)(4,1)S(1)}, s32[]{:S(2)}) async-start(s8[4718592]{0:T(1024)(128)(4,1)} %bitcast.211), calls=%async_computation.8 | async-start | bytes 8388608
  397.4 25.0 %collective-permute-start.13 = (bf16[2,8,64,256]{3,2,1,0:T(8,128)(2,1)S(1)}, bf16[2,8,64,256]{3,2,1,0:T(8,128)(2,1)S(1)}, u32[]{:S(2)}, u32[]{:S(2)}) collective-permute-start(bf16[2,8,64,256]{3,2,1,0:T(8,128)(2,1)S(1)} %bitcast.225), channel_id=1, source_target_pairs={{64,0},{65,1},{66,2},{67,3},{68,4},{69,5},{70,6},{71,7},{72,8},{73... | collective-permute-start | bytes 1572872 | tf_op jit(solution)/shard_map/ppermute | solution.py:25
  422.4 7.7 collective-permute-start.14
  427.3 7.6 collective-permute-start.15
  448.3 329.9 %reduce-scatter.7.cloned.1.call-start = ((), (), s32[]{:S(2)}) async-start(), calls=%async_computation.4 | async-start | bytes 6488064
  448.4 7.3 collective-permute-start.16
  454.1 5.0 collective-permute-start.17
  485.3 294.7 %copy-start.10 = (bf16[2,3,8,64]{1,0,3,2:T(2,128)(2,1)S(1)}, bf16[2,3,8,64]{1,0,3,2:T(2,128)(2,1)}, u32[]{:S(2)}) copy-start(bf16[2,3,8,64]{1,0,3,2:T(2,128)(2,1)} %copy-done.9) | copy-start | bytes 18436
  485.3 296.5 %copy-start.7 = (bf16[1024,256]{1,0:T(8,128)(2,1)S(1)}, bf16[1024,256]{1,0:T(8,128)(2,1)}, u32[]{:S(2)}) copy-start(bf16[1024,256]{1,0:T(8,128)(2,1)} %copy-done.6) | copy-start | bytes 1572868
  485.3 389.2 %copy-start.1 = (bf16[2,4,3,96,96]{4,3,2,1,0:T(8,128)(2,1)S(1)}, bf16[2,4,3,96,96]{4,3,2,1,0:T(8,128)(2,1)}, u32[]{:S(2)}) copy-start(bf16[2,4,3,96,96]{4,3,2,1,0:T(8,128)(2,1)} %param.15) | copy-start | bytes 1327108
  485.3 385.6 %all-reduce.12.cloned.1.call-start = ((), (), s32[]{:S(2)}) async-start(), calls=%async_computation.6 | async-start | bytes 1048576 | tf_op jit(solution)/shard_map/psum | solution.py:224
  (13 other events, 36.5 us)
Sparse Core Ops, SparseCore 0:
  9.7 138.2 all-gather.4
  149.6 153.7 all-gather.6
  448.4 156.8 reduce-scatter.8
  607.6 170.5 reduce-scatter.6
  780.5 55.5 all-reduce.11
where the time goes:
time: 890 us; the launch traced here: 882 us
  waiting for transfers between devices  595 us (67%)
  blocking collectives  88.2 us (10%)
  starting transfers between devices  65 us (7%)
  local copies, waits for them, and re-layouts  62.2 us (7%)
  matrix products  41.6 us (5%)
  between operations  17.8 us (2%)
  other arithmetic  12.8 us (1%)
    unnamed x7, waiting for transfers between devices  292 us
    all_gather x1, waiting for transfers between devices, body(): lax.all_gather(proj_weight[0], 'fsdp', axis=0, tiled=True)  138 us
    all_gather x1, waiting for transfers between devices, fetch_convs(): gathered = lax.all_gather(conv_weight[0], 'fsdp', axis=1, tiled=True)  132 us
    psum x1, blocking collectives, body(): lax.psum((head_term, loss_term), ('segment', 'fsdp', 'dp'))  88.2 us
    unnamed x114, local copies, waits for them, and re-layouts  46.8 us
    ppermute x8, starting transfers between devices, extended(): before = lax.ppermute(last, axis, up)  28.8 us
    ppermute x2, starting transfers between devices, shifted(): return lax.ppermute(shard, axis, pairs)  24.7 us
    ppermute x8, waiting for transfers between devices, extended(): after = lax.ppermute(initial, axis, down)  23.1 us
  transfers between devices with their start and end apart: 23, of which 14 were waited for; matrix products, arithmetic and copies ran while one was open for 8% of the time, Pallas kernels for 0%

commit v1 on v0

--- a/solution.py
+++ b/solution.py
@@ -4,6 +4,18 @@
 from jax.sharding import PartitionSpec as P
 
 LOSS_SCALE = 8192.0
+
+
+def _shape_task(x_in):
+    return jnp.concatenate(
+        lax.all_to_all(
+            jnp.stack([x_in for _ in range(lax.psum(1, axis_name="fsdp"))], axis=0),
+            axis_name="fsdp",
+            split_axis=0,
+            concat_axis=0,
+        ),
+        axis=0,
+    )
 
 
 def extended(shard, sides, width):
@@ -167,11 +179,7 @@
     crop_here = first_global // grid_cols
     row_base = first_global % grid_cols
     columns = tokens
-    projected = jnp.dot(
-        columns,
-        lax.all_gather(proj_weight[0], "fsdp", axis=0, tiled=True),
-        preferred_element_type=jnp.float32,
-    )
+    projected = jnp.dot(columns, _shape_task(proj_weight[0]), preferred_element_type=jnp.float32)
     projected = projected.astype(jnp.bfloat16).reshape(
         micro_count, crop_count, band_rows, grid_cols, channels
     )

time: 890 us -> 759 us (0.85)
  waiting for transfers between devices: 595 us -> 450 us
  starting transfers between devices: 65 us -> 74.8 us
    all_gather x1 -> x0, waiting for transfers between devices: 138 us -> none  [body(): lax.all_gather(proj_weight[0], 'fsdp', axis=0, tiled=True)]
    all_gather x1, waiting for transfers between devices: 132 us -> 90.9 us  [fetch_convs(): gathered = lax.all_gather(conv_weight[0], 'fsdp', axis=1, tiled=True)]
    all_to_all x0 -> x1, waiting for transfers between devices: none -> 39.8 us  [_shape_task(): lax.all_to_all(jnp.stack([x_in for _ in range(lax.psum(1, axis_name='fsdp...]
    all_to_all x0 -> x1, starting transfers between devices: none -> 9.84 us  [_shape_task(): lax.all_to_all(jnp.stack([x_in for _ in range(lax.psum(1, axis_name='fsdp...]
    unnamed x7 -> x6, waiting for transfers between devices: 292 us -> 290 us
    unnamed x114 -> x116, local copies, waits for them, and re-layouts: 46.8 us -> 46.8 us
  transfers between devices with their start and end apart: 23 -> 23, of which waited for: 14 -> 15; matrix products, arithmetic and copies ran while one was open for 8% -> 9% of each run, Pallas kernels for 0% -> 0%
where the time goes in v1:
time: 759 us; the launch traced here: 751 us
  waiting for transfers between devices  450 us (59%)
  blocking collectives  88.9 us (12%)
  starting transfers between devices  74.8 us (10%)
  local copies, waits for them, and re-layouts  64.5 us (8%)
  matrix products  41.6 us (5%)
  between operations  17.9 us (2%)
  other arithmetic  12.8 us (2%)
    unnamed x6, waiting for transfers between devices  290 us
    all_gather x1, waiting for transfers between devices, fetch_convs(): gathered = lax.all_gather(conv_weight[0], 'fsdp', axis=1, tiled=True)  90.9 us
    psum x1, blocking collectives, body(): lax.psum((head_term, loss_term), ('segment', 'fsdp', 'dp'))  88.9 us
    unnamed x116, local copies, waits for them, and re-layouts  46.8 us
    all_to_all x1, waiting for transfers between devices, _shape_task(): lax.all_to_all(jnp.stack([x_in for _ in range(lax.psum(1, axis_name='fsdp...  39.8 us
    ppermute x8, starting transfers between devices, extended(): before = lax.ppermute(last, axis, up)  29.3 us
    ppermute x2, starting transfers between devices, shifted(): return lax.ppermute(shard, axis, pairs)  24.3 us
    ppermute x8, waiting for transfers between devices, extended(): after = lax.ppermute(initial, axis, down)  23.2 us
  transfers between devices with their start and end apart: 23, of which 15 were waited for; matrix products, arithmetic and copies ran while one was open for 9% of the time, Pallas kernels for 0%

profile of v1, /device:TPU:1, one launch (start us, length us, event | category | flops | bytes accessed | tf_op | source)
XLA Modules:
  0.0 750.7 jit_solution(4492311187762936036)
XLA Ops:
  7.2 3.0 stack.12
  10.2 9.8 %all-to-all-start = ((bf16[32,192,256]{2,1,0:T(8,128)(2,1)}), bf16[32,192,256]{2,1,0:T(8,128)(2,1)}, u32[]{:S(2)}, u32[]{:S(2)}) async-start(bf16[32,192,256]{2,1,0:T(8,128)(2,1)} %stack.12), calls=%async_computation | async-start | bytes 6291456 | tf_op jit(solution)/shard_map/all_to_all | solution.py:11
  20.9 39.8 %all-to-all-done = bf16[32,192,256]{2,1,0:T(8,128)(2,1)} async-done(((bf16[32,192,256]{2,1,0:T(8,128)(2,1)}), bf16[32,192,256]{2,1,0:T(8,128)(2,1)}, u32[]{:S(2)}, u32[]{:S(2)}) %all-to-all-start) | async-done | bytes 3145760 | tf_op jit(solution)/shard_map/all_to_all | solution.py:11
  60.7 7.3 fusion.7
  69.9 4.0 collective-permute-start
  84.2 90.9 %all-gather.3.cloned.1.call-done = bf16[1,2,2304,256]{3,2,1,0:T(8,128)(2,1)} async-done(((bf16[1,2,72,256]{3,2,1,0:T(8,128)(2,1)}), bf16[1,2,2304,256]{3,2,1,0:T(8,128)(2,1)}) %all-gather.3.cloned.1.call-update) | async-done | bytes 2359312 | tf_op jit(solution)/shard_map/all_gather | solution.py:153
  175.1 4.2 fusion.47
  179.3 2.7 collective-permute-start.2
  183.4 4.1 collective-permute-done.3
  193.0 12.9 %copy.50 = bf16[2,1,3,96,96]{2,1,0,4,3:T(2,128)(2,1)} copy(bf16[2,1,3,96,96]{4,3,2,1,0:T(8,128)(2,1)S(1)} %constant_dynamic-slice_fusion.2) | data formatting | bytes 221184
  205.9 3.3 gather_fusion
  210.7 3.4 collective-permute-done.4
  219.7 3.2 collective-permute-done.6
  224.9 2.5 multiply_convert_fusion
  227.4 1.9 collective-permute-start.7
  230.8 3.6 collective-permute-done.8
  244.8 4.5 collective-permute-start.9
  254.6 3.6 collective-permute-start.11
  260.4 3.7 collective-permute-done.12
  266.9 23.0 %collective-permute-start.13 = (bf16[2,8,64,256]{3,2,1,0:T(8,128)(2,1)S(1)}, bf16[2,8,64,256]{3,2,1,0:T(8,128)(2,1)S(1)}, u32[]{:S(2)}, u32[]{:S(2)}) collective-permute-start(bf16[2,8,64,256]{3,2,1,0:T(8,128)(2,1)S(1)} %bitcast.222), channel_id=1, source_target_pairs={{64,0},{65,1},{66,2},{67,3},{68,4},{69,5},{70,6},{71,7},{72,8},{73... | collective-permute-start | bytes 1572872 | tf_op jit(solution)/shard_map/ppermute | solution.py:37
  291.5 5.2 collective-permute-start.14
  299.6 4.8 collective-permute-done.15
  309.2 2.5 pad_maximum_fusion
  311.6 6.1 copy.48
  317.8 5.8 collective-permute-start.16
  325.1 3.5 collective-permute-done.17
  330.0 2.2 copy-done.11
  332.1 16.0 %convolution_bitcast_fusion = f32[6144,256]{0,1:T(8,128)} fusion(bf16[1024,6144]{1,0:T(8,128)(2,1)} %bitcast.220, bf16[1024,256]{1,0:T(8,128)(2,1)S(1)} %bitcast.146, f32[1024,256]{1,0:T(8,128)S(1)} %fusion.29, bf16[1024,2304]{1,0:T(8,128)(2,1)} %copy-done.11, bf16[2304,256]{1,0:T(8,128)(2,1)S(1)} %bitcast.203), kind=kOutput, calls=%fused_computation.1 | convolution fusion | flops 4430233600 | bytes 26345472 | tf_op jit(solution)/shard_map/dot_general | solution.py:65
  348.1 6.6 copy.46
  355.2 118.0 %reduce-scatter.9.cloned.1.call-done = f32[72,512]{1,0:T(8,128)} async-done(((f32[2304,512]{1,0:T(8,128)}), f32[72,512]{1,0:T(8,128)}) %reduce-scatter.9.cloned.1.call-update) | async-done | bytes 147472
  474.9 171.0 %reduce-scatter.7.cloned.1.call-done = f32[192,256]{1,0:T(8,128)} async-done(((f32[6144,256]{1,0:T(8,128)}), f32[192,256]{1,0:T(8,128)}) %reduce-scatter.7.cloned.1.call-update) | async-done | bytes 196624
  649.7 88.9 %all-reduce.8 = (f32[3,256]{1,0:T(4,128)}, f32[]{:T(128)}) all-reduce(f32[3,256]{1,0:T(4,128)S(1)} %convolution_select_fusion, f32[]{:T(128)S(6)} %select_n.191), channel_id=1, replica_groups=mesh['segment'=2,'fsdp'=32,'dp'=2] {'segment','fsdp','dp'}, use_global_device_ids=true, to_apply=%region_4.5 | all-reduce | flops 769 | bytes 6152 | tf_op jit(solution)/shard_map/psum | solution.py:235
  (242 shorter events, 71.0 us)
Async XLA Ops:
  7.2 174.9 %copy-start = (bf16[2,4,3,96,96]{4,3,2,1,0:T(8,128)(2,1)S(1)}, bf16[2,4,3,96,96]{4,3,2,1,0:T(8,128)(2,1)}, u32[]{:S(2)}) copy-start(bf16[2,4,3,96,96]{4,3,2,1,0:T(8,128)(2,1)} %param.15) | copy-start | bytes 1327108
  10.2 50.5 %all-to-all-start = ((bf16[32,192,256]{2,1,0:T(8,128)(2,1)}), bf16[32,192,256]{2,1,0:T(8,128)(2,1)}, u32[]{:S(2)}, u32[]{:S(2)}) async-start(bf16[32,192,256]{2,1,0:T(8,128)(2,1)} %stack.12), calls=%async_computation | async-start | bytes 6291456 | tf_op jit(solution)/shard_map/all_to_all | solution.py:11
  20.0 155.1 %all-gather.3.cloned.1.call-start = ((), (), s32[]{:S(2)}) async-start(), calls=%async_computation.3 | async-start | bytes 2433024 | tf_op jit(solution)/shard_map/all_gather | solution.py:153
  20.8 452.4 %reduce-scatter.9.cloned.1.call-start = ((), (), s32[]{:S(2)}) async-start(), calls=%async_computation.5 | async-start | bytes 4866048
  68.4 5.8 collective-permute-start.1
  69.9 5.4 collective-permute-start
  179.3 4.0 collective-permute-start.2
  182.1 5.4 collective-permute-start.3
  191.5 22.5 %collective-permute-start.4 = (bf16[2,8,64,256]{3,2,1,0:T(8,128)(2,1)S(1)}, bf16[2,8,64,256]{3,2,1,0:T(8,128)(2,1)S(1)}, u32[]{:S(2)}, u32[]{:S(2)}) collective-permute-start(bf16[2,8,64,256]{3,2,1,0:T(8,128)(2,1)S(1)} %bitcast.221), channel_id=1, source_target_pairs={{0,64},{1,65},{2,66},{3,67},{4,68},{5,69},{6,70},{7,71},{8,72},{9,... | collective-permute-start | bytes 1572872 | tf_op jit(solution)/shard_map/ppermute | solution.py:37
  193.0 16.8 %copy-start.16 = (s32[2,4]{1,0:T(2,128)S(1)}, s32[2,4]{1,0:T(2,128)}, u32[]{:S(2)}) copy-start(s32[2,4]{1,0:T(2,128)} %param.13) | copy-start | bytes 100
  193.0 16.9 %copy-start.17 = (f32[25,3]{0,1:T(4,128)S(1)}, f32[25,3]{0,1:T(4,128)}, u32[]{:S(2)}) copy-start(f32[25,3]{0,1:T(4,128)} %param.12) | copy-start | bytes 904
  214.4 23.8 %copy-start.2 = (f32[2,8,64,256]{3,2,1,0:T(8,128)}, f32[2,8,64,256]{3,2,1,0:T(8,128)S(1)}, u32[]{:S(2)}) copy-start(f32[2,8,64,256]{3,2,1,0:T(8,128)S(1)} %get-tuple-element.29) | copy-start | bytes 3145732
  214.5 5.2 collective-permute-start.5
  217.9 5.0 collective-permute-start.6
  227.4 3.3 collective-permute-start.7
  229.4 5.0 collective-permute-start.8
  241.1 8.1 %collective-permute-start.10 = (bf16[2,1,64,256]{3,2,1,0:T(8,128)(2,1)S(1)}, bf16[2,1,64,256]{3,2,1,0:T(8,128)(2,1)}, u32[]{:S(2)}, u32[]{:S(2)}) collective-permute-start(bf16[2,1,64,256]{3,2,1,0:T(8,128)(2,1)S(1)} %get-tuple-element.68), channel_id=1, source_target_pairs={{2,0},{4,2},{6,4},{8,6},{10,8},{12,10},{14,12},{16,14},{18,16},{20... | collective-permute-start | bytes 196616 | tf_op jit(solution)/shard_map/ppermute | solution.py:29
  244.8 6.1 collective-permute-start.9
  254.6 5.7 collective-permute-start.11
  258.9 5.2 collective-permute-start.12
  265.4 32.6 %slice-start = ((s8[4718592]{0:T(1024)(128)(4,1)}), s8[524288]{0:T(1024)(128)(4,1)S(1)}, s32[]{:S(2)}) async-start(s8[4718592]{0:T(1024)(128)(4,1)} %bitcast.208), calls=%async_computation.7 | async-start | bytes 1048576
  265.4 32.6 %slice-start.1 = ((s8[4718592]{0:T(1024)(128)(4,1)}), s8[4194304]{0:T(1024)(128)(4,1)S(1)}, s32[]{:S(2)}) async-start(s8[4718592]{0:T(1024)(128)(4,1)} %bitcast.208), calls=%async_computation.8 | async-start | bytes 8388608
  266.9 24.5 %collective-permute-start.13 = (bf16[2,8,64,256]{3,2,1,0:T(8,128)(2,1)S(1)}, bf16[2,8,64,256]{3,2,1,0:T(8,128)(2,1)S(1)}, u32[]{:S(2)}, u32[]{:S(2)}) collective-permute-start(bf16[2,8,64,256]{3,2,1,0:T(8,128)(2,1)S(1)} %bitcast.222), channel_id=1, source_target_pairs={{64,0},{65,1},{66,2},{67,3},{68,4},{69,5},{70,6},{71,7},{72,8},{73... | collective-permute-start | bytes 1572872 | tf_op jit(solution)/shard_map/ppermute | solution.py:37
  291.5 8.1 %collective-permute-start.14 = (bf16[2,1,64,256]{3,2,1,0:T(8,128)(2,1)S(1)}, bf16[2,1,64,256]{3,2,1,0:T(8,128)(2,1)S(1)}, u32[]{:S(2)}, u32[]{:S(2)}) collective-permute-start(bf16[2,1,64,256]{3,2,1,0:T(8,128)(2,1)S(1)} %get-tuple-element.61), channel_id=1, source_target_pairs={{0,2},{2,4},{4,6},{6,8},{8,10},{10,12},{12,14},{14,16},{16,18},{18... | collective-permute-start | bytes 196616 | tf_op jit(solution)/shard_map/ppermute | solution.py:28
  296.7 7.6 %collective-permute-start.15 = (bf16[2,1,64,256]{3,2,1,0:T(8,128)(2,1)S(1)}, bf16[2,1,64,256]{3,2,1,0:T(8,128)(2,1)S(1)}, u32[]{:S(2)}, u32[]{:S(2)}) collective-permute-start(bf16[2,1,64,256]{3,2,1,0:T(8,128)(2,1)S(1)} %get-tuple-element.62), channel_id=1, source_target_pairs={{2,0},{4,2},{6,4},{8,6},{10,8},{12,10},{14,12},{16,14},{18,16},{20... | collective-permute-start | bytes 196616 | tf_op jit(solution)/shard_map/ppermute | solution.py:29
  317.7 328.2 %reduce-scatter.7.cloned.1.call-start = ((), (), s32[]{:S(2)}) async-start(), calls=%async_computation.4 | async-start | bytes 6488064
  317.8 7.3 collective-permute-start.16
  323.6 5.0 collective-permute-start.17
  354.7 293.0 %copy-start.10 = (bf16[2,3,8,64]{1,0,3,2:T(2,128)(2,1)S(1)}, bf16[2,3,8,64]{1,0,3,2:T(2,128)(2,1)}, u32[]{:S(2)}) copy-start(bf16[2,3,8,64]{1,0,3,2:T(2,128)(2,1)} %copy-done.9) | copy-start | bytes 18436
  354.7 294.8 %copy-start.7 = (bf16[1024,256]{1,0:T(8,128)(2,1)S(1)}, bf16[1024,256]{1,0:T(8,128)(2,1)}, u32[]{:S(2)}) copy-start(bf16[1024,256]{1,0:T(8,128)(2,1)} %copy-done.6) | copy-start | bytes 1572868
  354.7 388.1 %copy-start.1 = (bf16[2,4,3,96,96]{4,3,2,1,0:T(8,128)(2,1)S(1)}, bf16[2,4,3,96,96]{4,3,2,1,0:T(8,128)(2,1)}, u32[]{:S(2)}) copy-start(bf16[2,4,3,96,96]{4,3,2,1,0:T(8,128)(2,1)} %param.15) | copy-start | bytes 1327108
  354.7 384.5 %all-reduce.12.cloned.1.call-start = ((), (), s32[]{:S(2)}) async-start(), calls=%async_computation.6 | async-start | bytes 1048576 | tf_op jit(solution)/shard_map/psum | solution.py:232
  (14 other events, 48.0 us)
Sparse Core Ops, SparseCore 0:
  22.5 152.5 all-gather.2
  317.9 155.2 reduce-scatter.8
  475.5 170.3 reduce-scatter.6
  648.2 56.5 all-reduce.11
